TPU v7x, 256 devices: a whole 4x4x8 slice. The times are simulated.
256 devices in a mesh: gx: 16 (over y, x), gy: 16 (over z, core).
Axes of the slice: x: 4, y: 4, z: 8, core: 2. Of those that a mesh axis runs over, the one named last changes fastest.
Arguments:
- vectors: float32 [8, 128, 256, 256], P(None, 'gx', 'gy'), may hold values from -10 to 10
- weight_x: float32 [128, 256, 256], P('gx', 'gy'), may hold values from 0.05 to 1
- weight_y: float32 [128, 256, 256], P('gx', 'gy'), may hold values from 0.05 to 1
- weight_z: float32 [128, 256, 256], P('gx', 'gy'), may hold values from 0.05 to 1
Outputs:
- refined: float32 [8, 128, 256, 256], P(None, 'gx', 'gy')
- eigenvalues: float32 [8], replicated
All inputs are finite; a program needn't handle non-finite values.
Results may differ from a plain program's by a relative error of at most 0.000075.
Values sent between devices are 32-bit elements; how exact they have to be, the bound alone decides.
No kernel may reach another device: no remote copies, remote signals or barrier semaphores. Data moves between devices by JAX's collectives and lax.ppermute only.
A program may use at most 128 MiB of HBM per device.

v0:
```python
import jax
import jax.numpy as jnp
from jax import lax
from jax.sharding import PartitionSpec as P

COARSE_SWEEPS = 4
OMEGA = 0.8
SHIFT = 0.1


def shifted(shard, axis, by):
    count = lax.axis_size(axis)
    pairs = [(i, i + by) for i in range(count) if 0 <= i + by < count]
    return lax.ppermute(shard, axis, pairs)


def with_halo(cells, sides, width):
    for axis, dim in sides:
        count = lax.axis_size(axis)
        ends = count - 1
        head = lax.slice_in_dim(cells, 0, width, axis=dim)
        tail = lax.slice_in_dim(cells, cells.shape[dim] - width, cells.shape[dim], axis=dim)
        cells = jnp.concatenate(
            [
                lax.ppermute(tail, axis, [(i, (i + 1) % count) for i in range(ends)]),
                cells,
                lax.ppermute(head, axis, [((i + 1) % count, i) for i in range(ends)]),
            ],
            axis=dim,
        )
    return cells


def lower_x(weights):
    rim = shifted(weights[-1:], "gx", 1)
    return jnp.concatenate([rim, weights[:-1]], 0)


def lower_y(weights):
    rim = shifted(weights[:, -1:], "gy", 1)
    return jnp.concatenate([rim, weights[:, :-1]], 1)


def lower_z(weights):
    return jnp.concatenate([jnp.zeros_like(weights[:, :, :1]), weights[:, :, :-1]], 2)


def trimmed(array):
    return array[..., 1:-1, 1:-1, :]


def inner_sum(field, parts):
    wx, lx, wy, ly, wz, lz = parts
    centre = trimmed(field)
    zpadded = jnp.pad(centre, ((0, 0), (0, 0), (0, 0), (1, 1)))
    total = wx[None] * field[:, 2:, 1:-1] + lx[None] * field[:, :-2, 1:-1]
    total = total + wy[None] * field[:, 1:-1, 2:] + ly[None] * field[:, 1:-1, :-2]
    total = total + wz[None] * zpadded[..., 2:] + lz[None] * zpadded[..., :-2]
    return total


def neighbours(field, parts, level):
    if level == "fine":
        padded = with_halo(field, (("gx", 1), ("gy", 2)), 1)
    else:
        padded = with_halo(field, (("gx", 1), ("gy", 2)), 1)
    return inner_sum(padded, parts)


def jacobi(guess, source, diag, parts, level):
    return (
        guess
        + OMEGA * (source - (diag[None] * guess - neighbours(guess, parts, level))) / diag[None]
    )


def rayleigh_sums(vectors, applied, degree):
    return lax.psum(
        (
            jnp.sum(vectors * applied, axis=(1, 2, 3)),
            jnp.sum(vectors * (degree[None] * vectors), axis=(1, 2, 3)),
        ),
        ("gx", "gy"),
    )


def coarse_weights(wx, wy, wz, degree):
    sx, sy, sz = wx.shape
    shape = (sx // 2, 2, sy // 2, 2, sz // 2, 2)
    cx = wx.reshape(shape)[:, 1].sum(axis=(2, 4))
    cy = wy.reshape(shape)[:, :, :, 1].sum(axis=(1, 4))
    cz = wz.reshape(shape)[..., 1].sum(axis=(1, 3))
    dsum = degree.reshape(shape).sum(axis=(1, 3, 5))
    return (cx, cy, cz, dsum)


def restrict(field):
    kk, sx, sy, sz = field.shape
    return field.reshape(kk, sx // 2, 2, sy // 2, 2, sz // 2, 2).sum(axis=(2, 4, 6))


def prolong(field):
    kk, sx, sy, sz = field.shape
    return jnp.broadcast_to(field[:, :, None, :, None, :, None], (kk, sx, 2, sy, 2, sz, 2)).reshape(
        kk, 2 * sx, 2 * sy, 2 * sz
    )


def per_device(vectors, weight_x, weight_y, weight_z):
    local_x, local_y, depth = weight_x.shape
    span_x = local_x * lax.axis_size("gx")
    span_y = local_y * lax.axis_size("gy")
    pos_x = lax.axis_index("gx") * local_x + lax.broadcasted_iota(jnp.int32, (local_x, 1, 1), 0)
    pos_y = lax.axis_index("gy") * local_y + lax.broadcasted_iota(jnp.int32, (1, local_y, 1), 1)
    pos_z = lax.broadcasted_iota(jnp.int32, (1, 1, depth), 2)
    wx = jnp.where(pos_x < span_x - 1, weight_x, jnp.zeros_like(weight_x))
    wy = jnp.where(pos_y < span_y - 1, weight_y, jnp.zeros_like(weight_y))
    wz = jnp.where(pos_z < depth - 1, weight_z, jnp.zeros_like(weight_z))
    parts = (wx, lower_x(wx), wy, lower_y(wy), wz, lower_z(wz))
    degree = parts[0] + parts[1] + parts[2] + parts[3] + parts[4] + parts[5]
    applied = degree[None] * vectors - neighbours(vectors, parts, "fine")
    numer, denom = rayleigh_sums(vectors, applied, degree)
    eigenvalues = numer / denom
    resid = applied - eigenvalues[:, None, None, None] * (degree[None] * vectors)
    dfine = (1.0 + SHIFT) * degree
    guess = OMEGA * resid / dfine[None]
    guess = jacobi(guess, resid, dfine, parts, "fine")
    fine_rest = resid - (dfine[None] * guess - neighbours(guess, parts, "fine"))
    cx, cy, cz, dsum = coarse_weights(wx, wy, wz, degree)
    cparts = (cx, lower_x(cx), cy, lower_y(cy), cz, lower_z(cz))
    dcoarse = cparts[0] + cparts[1] + cparts[2] + cparts[3] + cparts[4] + cparts[5] + SHIFT * dsum
    rcoarse = restrict(fine_rest)
    correction = OMEGA * rcoarse / dcoarse[None]
    for sweep in range(COARSE_SWEEPS - 1):
        correction = jacobi(correction, rcoarse, dcoarse, cparts, "coarse")
    guess = guess + prolong(correction)
    guess = jacobi(guess, resid, dfine, parts, "fine")
    updated = vectors - guess
    local_gram = jnp.einsum(
        "aijk,bijk->ab", updated, degree[None] * updated, precision=lax.Precision.HIGHEST
    )
    gram = lax.psum(local_gram, ("gx", "gy"))
    gram = gram / (span_x * span_y * depth)
    chol = jnp.linalg.cholesky(gram)
    flat = updated.reshape(updated.shape[0], -1)
    refined = jax.scipy.linalg.solve_triangular(chol, flat, lower=True).reshape(updated.shape)
    return (refined, eigenvalues)


def solution(mesh):
    return jax.shard_map(
        per_device,
        mesh=mesh,
        in_specs=(
            P(None, "gx", "gy", None),
            P("gx", "gy", None),
            P("gx", "gy", None),
            P("gx", "gy", None),
        ),
        out_specs=(P(None, "gx", "gy", None), P()),
        check_vma=False,
    )
```

profile of v0, /device:TPU:1, one launch (start us, length us, event | category | flops | bytes accessed | tf_op | source)
XLA Modules:
  0.0 427.5 jit_solution(8508537190117706973)
XLA Ops:
  1.7 3.9 collective-permute-start
  6.6 4.4 %collective-permute-start.1 = (f32[8,1,256]{2,1,0:T(1,128)S(1)}, f32[8,1,256]{2,1,0:T(1,128)S(1)}, u32[]{:S(2)}, u32[]{:S(2)}) collective-permute-start(f32[8,1,256]{2,1,0:T(1,128)S(1)} %slice.374), channel_id=1, source_target_pairs={{0,1},{1,2},{2,3},{3,4},{4,5},{5,6},{6,7},{7,8},{8,9},{9,10},{10,1... | collective-permute-start | bytes 24584 | tf_op jit(solution)/shard_map/ppermute | solution.py:14
  12.0 3.1 collective-permute-start.3
  15.2 1.3 collective-permute-start.2
  16.5 9.8 %reshape.74 = f32[4,2,8,2,128,2]{5,4,3,2,1,0:T(8,128)} reshape(f32[8,16,256]{2,1,0:T(8,128)S(1)} %broadcast_select_fusion.2) | data formatting | bytes 262144 | tf_op jit(solution)/shard_map/reshape | solution.py:90
  26.6 1.9 collective-permute-start.4
  28.6 3.6 collective-permute-start.5
  33.8 2.1 fusion
  35.9 82.2 %all-reduce.9 = (f32[8]{0:T(128)S(1)}, f32[8]{0:T(128)S(1)}) all-reduce(f32[8]{0:T(128)S(1)} %get-tuple-element.19, f32[8]{0:T(128)S(1)} %get-tuple-element.18), channel_id=1, replica_groups=mesh['gx'=16,'gy'=16] {'gx','gy'}, use_global_device_ids=true, to_apply=%region_1.2 | all-reduce | flops 16 | bytes 128 | tf_op jit(solution)/shard_map/psum | solution.py:78
  118.1 1.7 multiply_divide_fusion
  120.6 1.3 collective-permute-start.6
  121.8 4.7 %collective-permute-start.7 = (f32[8,1,16,256]{3,2,1,0:T(8,128)}, f32[8,1,16,256]{3,2,1,0:T(8,128)}, u32[]{:S(2)}, u32[]{:S(2)}) collective-permute-start(f32[8,1,16,256]{3,2,1,0:T(8,128)} %get-tuple-element.44), channel_id=1, source_target_pairs={{0,16},{16,32},{32,48},{48,64},{64,80},{80,96},{96,112},{112,128},... | collective-permute-start | bytes 393224 | tf_op jit(solution)/shard_map/ppermute | solution.py:25
  126.5 2.8 slice_reduce_fusion.2
  130.5 2.5 collective-permute-start.14
  133.0 9.7 %reshape.75 = f32[4,2,8,2,128,2]{5,4,3,2,1,0:T(8,128)} reshape(f32[8,16,256]{2,1,0:T(8,128)S(1)} %broadcast_select_fusion.1) | data formatting | bytes 262144 | tf_op jit(solution)/shard_map/reshape | solution.py:91
  142.7 1.0 pad_maximum_fusion.62
  143.8 3.4 collective-permute-start.8
  147.2 2.9 collective-permute-start.9
  150.1 2.8 slice_reduce_fusion.1
  153.5 2.5 collective-permute-start.15
  156.1 9.8 %reshape.76 = f32[4,2,8,2,128,2]{5,4,3,2,1,0:T(8,128)} reshape(f32[8,16,256]{2,1,0:T(8,128)S(1)} %broadcast_select_fusion) | data formatting | bytes 262144 | tf_op jit(solution)/shard_map/reshape | solution.py:92
  166.1 5.3 %fusion.13 = f32[8,8,16,256]{3,2,1,0:T(8,128)S(1)} fusion(f32[8,8,16,256]{3,2,1,0:T(8,128)} %copy-done.1, f32[8,8,16,256]{3,2,1,0:T(8,128)S(1)} %get-tuple-element.27, f32[8,10,1,256]{3,2,1,0:T(1,128)S(1)} %copy.441, f32[8,1,16,256]{3,2,1,0:T(8,128)} %copy-done.25, f32[8,1,16,256]{3,2,1,0:T(8,128)} %collective-permute-done.7, ...), kind=kLoop, calls=%fused_computation.28 | loop fusion | flops 6553600 | bytes 4489216 | tf_op jit(solution)/shard_map/add | solution.py:72
  172.1 1.3 collective-permute-start.10
  173.4 4.7 %collective-permute-start.11 = (f32[8,1,16,256]{3,2,1,0:T(8,128)}, f32[8,1,16,256]{3,2,1,0:T(8,128)}, u32[]{:S(2)}, u32[]{:S(2)}) collective-permute-start(f32[8,1,16,256]{3,2,1,0:T(8,128)} %get-tuple-element.42), channel_id=1, source_target_pairs={{0,16},{16,32},{32,48},{48,64},{64,80},{80,96},{96,112},{112,128},... | collective-permute-start | bytes 393224 | tf_op jit(solution)/shard_map/ppermute | solution.py:25
  178.1 6.8 %slice_reduce_fusion = f32[4,8,128]{2,1,0:T(8,128)} fusion(f32[4,2,8,2,128,2]{5,4,3,2,1,0:T(8,128)} %reshape.76), kind=kLoop, calls=%fused_computation | loop fusion | flops 12288 | bytes 81920 | tf_op jit(solution)/shard_map/reduce_sum | solution.py:92
  184.8 10.5 %reshape.77 = f32[4,2,8,2,128,2]{5,4,3,2,1,0:T(8,128)} reshape(f32[8,16,256]{2,1,0:T(8,128)} %copy-done.8) | data formatting | bytes 262144 | tf_op jit(solution)/shard_map/reshape | solution.py:93
  195.3 4.6 %reduce_sum.69 = f32[4,8,128]{2,1,0:T(8,128)} reduce(f32[4,2,8,2,128,2]{5,4,3,2,1,0:T(8,128)} %reshape.77, f32[]{:T(128)} %constant.65.clone.1), dimensions={1,3,5}, to_apply=%region_8.9 | reduce | flops 28672 | bytes 147460 | tf_op jit(solution)/shard_map/reduce_sum | solution.py:93
  200.0 1.2 pad_maximum_fusion.59
  201.2 3.0 collective-permute-start.12
  204.3 2.5 collective-permute-start.13
  206.9 1.4 multiply_add_fusion
  208.5 2.8 fusion.19
  211.3 9.8 %copy.446 = f32[8,8,16,256]{0,3,2,1:T(8,128)} copy(f32[8,8,16,256]{3,2,1,0:T(8,128)} %fusion.19) | data formatting | bytes 2097152 | tf_op jit(solution)/shard_map/sub | solution.py:128
  221.1 13.1 %reduce_sum.65 = f32[8,4,8,128]{0,3,2,1:T(8,128)} reduce(f32[8,4,2,8,2,128,2]{0,6,5,4,3,2,1:T(2,128)} %bitcast.30, f32[]{:T(128)} %constant.65.clone.1), dimensions={2,4,6}, to_apply=%region_4.5 | reduce | flops 229376 | bytes 1179652 | tf_op jit(solution)/shard_map/reduce_sum | solution.py:99
  234.2 2.8 copy.447
  237.1 1.0 multiply_divide_fusion.1
  238.1 1.3 collective-permute-start.16
  239.4 4.0 collective-permute-start.17
  244.4 2.9 collective-permute-start.18
  247.4 4.3 %collective-permute-start.19 = (f32[8,6,1,128]{3,2,1,0:T(1,128)S(1)}, f32[8,6,1,128]{3,2,1,0:T(1,128)S(1)}, u32[]{:S(2)}, u32[]{:S(2)}) collective-permute-start(f32[8,6,1,128]{3,2,1,0:T(1,128)S(1)} %get-tuple-element.53), channel_id=1, source_target_pairs={{0,1},{1,2},{2,3},{3,4},{4,5},{5,6},{6,7},{7,8},{8,9},{9,10},{10,1... | collective-permute-start | bytes 73736 | tf_op jit(solution)/shard_map/ppermute | solution.py:25
  252.7 1.1 fusion.68
  253.8 1.3 collective-permute-start.20
  255.1 4.6 %collective-permute-start.21 = (f32[8,1,8,128]{3,2,1,0:T(8,128)S(1)}, f32[8,1,8,128]{3,2,1,0:T(8,128)S(1)}, u32[]{:S(2)}, u32[]{:S(2)}) collective-permute-start(f32[8,1,8,128]{3,2,1,0:T(8,128)S(1)} %get-tuple-element.56), channel_id=1, source_target_pairs={{0,16},{16,32},{32,48},{48,64},{64,80},{80,96},{96,112},{112,128},... | collective-permute-start | bytes 98312 | tf_op jit(solution)/shard_map/ppermute | solution.py:25
  260.7 1.9 collective-permute-start.22
  262.6 5.1 %collective-permute-start.23 = (f32[8,6,1,128]{3,2,1,0:T(1,128)S(1)}, f32[8,6,1,128]{3,2,1,0:T(1,128)S(1)}, u32[]{:S(2)}, u32[]{:S(2)}) collective-permute-start(f32[8,6,1,128]{3,2,1,0:T(1,128)S(1)} %get-tuple-element.51), channel_id=1, source_target_pairs={{0,1},{1,2},{2,3},{3,4},{4,5},{5,6},{6,7},{7,8},{8,9},{9,10},{10,1... | collective-permute-start | bytes 73736 | tf_op jit(solution)/shard_map/ppermute | solution.py:25
  268.8 1.3 collective-permute-start.24
  270.1 4.6 %collective-permute-start.25 = (f32[8,1,8,128]{3,2,1,0:T(8,128)S(1)}, f32[8,1,8,128]{3,2,1,0:T(8,128)S(1)}, u32[]{:S(2)}, u32[]{:S(2)}) collective-permute-start(f32[8,1,8,128]{3,2,1,0:T(8,128)S(1)} %get-tuple-element.54), channel_id=1, source_target_pairs={{0,16},{16,32},{32,48},{48,64},{64,80},{80,96},{96,112},{112,128},... | collective-permute-start | bytes 98312 | tf_op jit(solution)/shard_map/ppermute | solution.py:25
  275.8 1.9 collective-permute-start.26
  277.7 5.1 %collective-permute-start.27 = (f32[8,6,1,128]{3,2,1,0:T(1,128)S(1)}, f32[8,6,1,128]{3,2,1,0:T(1,128)S(1)}, u32[]{:S(2)}, u32[]{:S(2)}) collective-permute-start(f32[8,6,1,128]{3,2,1,0:T(1,128)S(1)} %get-tuple-element.49), channel_id=1, source_target_pairs={{0,1},{1,2},{2,3},{3,4},{4,5},{5,6},{6,7},{7,8},{8,9},{9,10},{10,1... | collective-permute-start | bytes 73736 | tf_op jit(solution)/shard_map/ppermute | solution.py:25
  284.5 2.9 copy.451
  287.4 7.1 %broadcast_in_dim.30 = f32[8,4,2,8,2,128,2]{0,6,5,4,3,2,1:T(2,128)} broadcast(f32[8,4,8,128]{0,3,2,1:T(8,128)} %copy.451), dimensions={0,1,3,5} | broadcast | bytes 1179648 | tf_op jit(solution)/shard_map/broadcast_in_dim | solution.py:104
  294.5 10.6 %copy.452 = f32[8,8,16,256]{3,2,1,0:T(8,128)} copy(f32[8,8,16,256]{0,3,2,1:T(8,128)} %bitcast.31) | data formatting | bytes 2097152 | tf_op jit(solution)/shard_map/reshape | solution.py:104
  305.1 1.4 add.263
  306.6 1.4 collective-permute-start.28
  308.1 4.6 %collective-permute-start.29 = (f32[8,1,16,256]{3,2,1,0:T(8,128)S(1)}, f32[8,1,16,256]{3,2,1,0:T(8,128)S(1)}, u32[]{:S(2)}, u32[]{:S(2)}) collective-permute-start(f32[8,1,16,256]{3,2,1,0:T(8,128)S(1)} %get-tuple-element.40), channel_id=1, source_target_pairs={{0,16},{16,32},{32,48},{48,64},{64,80},{80,96},{96,112},{112,128},... | collective-permute-start | bytes 393224 | tf_op jit(solution)/shard_map/ppermute | solution.py:25
  313.1 1.5 collective-permute-done.29
  314.7 1.9 collective-permute-start.30
  316.7 5.3 %collective-permute-start.31 = (f32[8,10,1,256]{3,0,2,1:T(8,128)S(1)}, f32[8,10,1,256]{3,0,2,1:T(8,128)S(1)}, u32[]{:S(2)}, u32[]{:S(2)}) collective-permute-start(f32[8,10,1,256]{3,0,2,1:T(8,128)S(1)} %copy.455), channel_id=1, source_target_pairs={{0,1},{1,2},{2,3},{3,4},{4,5},{5,6},{6,7},{7,8},{8,9},{9,10},{10,1... | collective-permute-start | bytes 245768 | tf_op jit(solution)/shard_map/ppermute | solution.py:25
  322.1 1.1 collective-permute-done.31
  323.3 1.6 broadcast_multiply_fusion
  324.9 3.0 convolution_bitcast_fusion
  327.9 93.9 %psum.23 = f32[8,8]{0,1:T(8,128)S(1)} all-reduce(f32[8,8]{0,1:T(8,128)S(1)} %convolution_bitcast_fusion), channel_id=1, replica_groups=mesh['gx'=16,'gy'=16] {'gx','gy'}, use_global_device_ids=true, to_apply=%region_9.10 | all-reduce | flops 64 | bytes 512 | tf_op jit(solution)/shard_map/psum | solution.py:142
  425.1 1.0 fusion.110
  426.2 1.3 copy.462
  (158 shorter events, 19.4 us)
Async XLA Ops:
  1.6 24.6 %copy-start.2 = (f32[8,16,256]{2,1,0:T(8,128)}, f32[8,16,256]{2,1,0:T(8,128)S(1)}, u32[]{:S(2)}) copy-start(f32[8,16,256]{2,1,0:T(8,128)S(1)} %broadcast_select_fusion.2) | copy-start | bytes 393220
  1.7 30.6 %collective-permute-start = (f32[1,16,256]{2,1,0:T(8,128)S(1)}, f32[1,16,256]{2,1,0:T(8,128)S(1)}, u32[]{:S(2)}, u32[]{:S(2)}) collective-permute-start(f32[1,16,256]{2,1,0:T(8,128)S(1)} %slice.372), channel_id=1, source_target_pairs={{0,16},{16,32},{32,48},{48,64},{64,80},{80,96},{96,112},{112,128},... | collective-permute-start | bytes 49160 | tf_op jit(solution)/shard_map/ppermute | solution.py:14
  6.6 25.6 %collective-permute-start.1 = (f32[8,1,256]{2,1,0:T(1,128)S(1)}, f32[8,1,256]{2,1,0:T(1,128)S(1)}, u32[]{:S(2)}, u32[]{:S(2)}) collective-permute-start(f32[8,1,256]{2,1,0:T(1,128)S(1)} %slice.374), channel_id=1, source_target_pairs={{0,1},{1,2},{2,3},{3,4},{4,5},{5,6},{6,7},{7,8},{8,9},{9,10},{10,1... | collective-permute-start | bytes 24584 | tf_op jit(solution)/shard_map/ppermute | solution.py:14
  12.0 14.3 %collective-permute-start.3 = (f32[8,1,16,256]{3,2,1,0:T(8,128)S(1)}, f32[8,1,16,256]{3,2,1,0:T(8,128)S(1)}, u32[]{:S(2)}, u32[]{:S(2)}) collective-permute-start(f32[8,1,16,256]{3,2,1,0:T(8,128)S(1)} %get-tuple-element.47), channel_id=1, source_target_pairs={{0,16},{16,32},{32,48},{48,64},{64,80},{80,96},{96,112},{112,128},... | collective-permute-start | bytes 393224 | tf_op jit(solution)/shard_map/ppermute | solution.py:25
  15.2 11.3 %collective-permute-start.2 = (f32[8,1,16,256]{3,2,1,0:T(8,128)S(1)}, f32[8,1,16,256]{3,2,1,0:T(8,128)S(1)}, u32[]{:S(2)}, u32[]{:S(2)}) collective-permute-start(f32[8,1,16,256]{3,2,1,0:T(8,128)S(1)} %get-tuple-element.46), channel_id=1, source_target_pairs={{16,0},{32,16},{48,32},{64,48},{80,64},{96,80},{112,96},{128,112},... | collective-permute-start | bytes 393224 | tf_op jit(solution)/shard_map/ppermute | solution.py:27
  16.5 9.8 %copy-start.26 = (f32[8,16,256]{2,1,0:T(8,128)S(1)}, f32[8,16,256]{2,1,0:T(8,128)}, u32[]{:S(2)}) copy-start(f32[8,16,256]{2,1,0:T(8,128)} %param.7) | copy-start | bytes 393220
  16.5 9.8 %copy-start = (f32[8,8,16,256]{3,2,1,0:T(8,128)S(1)}, f32[8,8,16,256]{3,2,1,0:T(8,128)}, u32[]{:S(2)}) copy-start(f32[8,8,16,256]{3,2,1,0:T(8,128)} %param.4) | copy-start | bytes 3145732
  26.3 5.9 %slice-start = ((f32[8,16,256]{2,1,0:T(8,128)}), f32[7,16,256]{2,1,0:T(8,128)S(1)}, s32[]{:S(2)}) async-start(f32[8,16,256]{2,1,0:T(8,128)} %copy-done.2), calls=%async_computation | async-start | bytes 229376 | tf_op jit(solution)/shard_map/slice | solution.py:36
  26.3 5.9 %copy-start.27 = (f32[8,16,256]{2,1,0:T(8,128)S(1)}, f32[8,16,256]{2,1,0:T(8,128)}, u32[]{:S(2)}) copy-start(f32[8,16,256]{2,1,0:T(8,128)} %param.5) | copy-start | bytes 393220
  26.3 5.9 %copy-start.28 = (f32[8,16,256]{2,1,0:T(8,128)S(1)}, f32[8,16,256]{2,1,0:T(8,128)}, u32[]{:S(2)}) copy-start(f32[8,16,256]{2,1,0:T(8,128)} %param.6) | copy-start | bytes 393220
  26.5 7.3 %copy-start.3 = (f32[8,16,256]{2,1,0:T(8,128)S(1)}, f32[8,16,256]{2,1,0:T(8,128)}, u32[]{:S(2)}) copy-start(f32[8,16,256]{2,1,0:T(8,128)} %copy-done.2) | copy-start | bytes 393220
  26.6 6.4 %collective-permute-start.4 = (f32[8,10,1,256]{3,0,2,1:T(8,128)S(1)}, f32[8,10,1,256]{3,0,2,1:T(8,128)S(1)}, u32[]{:S(2)}, u32[]{:S(2)}) collective-permute-start(f32[8,10,1,256]{3,0,2,1:T(8,128)S(1)} %copy.466), channel_id=1, source_target_pairs={{1,0},{2,1},{3,2},{4,3},{5,4},{6,5},{7,6},{8,7},{9,8},{10,9},{11,1... | collective-permute-start | bytes 245768 | tf_op jit(solution)/shard_map/ppermute | solution.py:27
  28.6 5.1 %collective-permute-start.5 = (f32[8,10,1,256]{3,0,2,1:T(8,128)S(1)}, f32[8,10,1,256]{3,0,2,1:T(8,128)S(1)}, u32[]{:S(2)}, u32[]{:S(2)}) collective-permute-start(f32[8,10,1,256]{3,0,2,1:T(8,128)S(1)} %copy.467), channel_id=1, source_target_pairs={{0,1},{1,2},{2,3},{3,4},{4,5},{5,6},{6,7},{7,8},{8,9},{9,10},{10,1... | collective-permute-start | bytes 245768 | tf_op jit(solution)/shard_map/ppermute | solution.py:25
  33.1 2.8 copy-start.17
  33.8 84.3 %copy-start.5 = (f32[8,16,256]{2,1,0:T(8,128)S(1)}, f32[8,16,256]{2,1,0:T(8,128)}, u32[]{:S(2)}) copy-start(f32[8,16,256]{2,1,0:T(8,128)} %get-tuple-element.28) | copy-start | bytes 393220
  119.8 22.9 %copy-start.1 = (f32[8,8,16,256]{3,2,1,0:T(8,128)}, f32[8,8,16,256]{3,2,1,0:T(8,128)S(1)}, u32[]{:S(2)}) copy-start(f32[8,8,16,256]{3,2,1,0:T(8,128)S(1)} %get-tuple-element.26) | copy-start | bytes 3145732
  120.6 22.2 %collective-permute-start.6 = (f32[8,1,16,256]{3,2,1,0:T(8,128)}, f32[8,1,16,256]{3,2,1,0:T(8,128)S(1)}, u32[]{:S(2)}, u32[]{:S(2)}) collective-permute-start(f32[8,1,16,256]{3,2,1,0:T(8,128)} %get-tuple-element.45), channel_id=1, source_target_pairs={{16,0},{32,16},{48,32},{64,48},{80,64},{96,80},{112,96},{128,112},... | collective-permute-start | bytes 393224 | tf_op jit(solution)/shard_map/ppermute | solution.py:27
  121.8 20.9 %collective-permute-start.7 = (f32[8,1,16,256]{3,2,1,0:T(8,128)}, f32[8,1,16,256]{3,2,1,0:T(8,128)}, u32[]{:S(2)}, u32[]{:S(2)}) collective-permute-start(f32[8,1,16,256]{3,2,1,0:T(8,128)} %get-tuple-element.44), channel_id=1, source_target_pairs={{0,16},{16,32},{32,48},{48,64},{64,80},{80,96},{96,112},{112,128},... | collective-permute-start | bytes 393224 | tf_op jit(solution)/shard_map/ppermute | solution.py:25
  130.5 76.3 %collective-permute-start.14 = (f32[1,8,128]{2,1,0:T(8,128)}, f32[1,8,128]{2,1,0:T(8,128)}, u32[]{:S(2)}, u32[]{:S(2)}) collective-permute-start(f32[1,8,128]{2,1,0:T(8,128)} %slice.384), channel_id=1, source_target_pairs={{0,16},{16,32},{32,48},{48,64},{64,80},{80,96},{96,112},{112,128},... | collective-permute-start | bytes 12296 | tf_op jit(solution)/shard_map/ppermute | solution.py:14
  142.7 10.2 %copy-start.25 = (f32[8,1,16,256]{3,2,1,0:T(8,128)}, f32[8,1,16,256]{3,2,1,0:T(8,128)S(1)}, u32[]{:S(2)}) copy-start(f32[8,1,16,256]{3,2,1,0:T(8,128)S(1)} %collective-permute-done.6) | copy-start | bytes 393220
  143.8 22.1 %collective-permute-start.8 = (f32[8,10,1,256]{3,0,2,1:T(8,128)S(1)}, f32[8,10,1,256]{3,0,2,1:T(8,128)S(1)}, u32[]{:S(2)}, u32[]{:S(2)}) collective-permute-start(f32[8,10,1,256]{3,0,2,1:T(8,128)S(1)} %copy.438), channel_id=1, source_target_pairs={{1,0},{2,1},{3,2},{4,3},{5,4},{6,5},{7,6},{8,7},{9,8},{10,9},{11,1... | collective-permute-start | bytes 245768 | tf_op jit(solution)/shard_map/ppermute | solution.py:27
  147.2 18.7 %collective-permute-start.9 = (f32[8,10,1,256]{3,0,2,1:T(8,128)S(1)}, f32[8,10,1,256]{3,0,2,1:T(8,128)S(1)}, u32[]{:S(2)}, u32[]{:S(2)}) collective-permute-start(f32[8,10,1,256]{3,0,2,1:T(8,128)S(1)} %copy.440), channel_id=1, source_target_pairs={{0,1},{1,2},{2,3},{3,4},{4,5},{5,6},{6,7},{7,8},{8,9},{9,10},{10,1... | collective-permute-start | bytes 245768 | tf_op jit(solution)/shard_map/ppermute | solution.py:25
  153.5 12.5 %copy-start.4 = (f32[8,16,256]{2,1,0:T(8,128)S(1)}, f32[8,16,256]{2,1,0:T(8,128)}, u32[]{:S(2)}) copy-start(f32[8,16,256]{2,1,0:T(8,128)} %copy-done.2) | copy-start | bytes 393220
  153.5 53.3 %collective-permute-start.15 = (f32[4,1,128]{2,1,0:T(1,128)}, f32[4,1,128]{2,1,0:T(1,128)}, u32[]{:S(2)}, u32[]{:S(2)}) collective-permute-start(f32[4,1,128]{2,1,0:T(1,128)} %slice.387), channel_id=1, source_target_pairs={{0,1},{1,2},{2,3},{3,4},{4,5},{5,6},{6,7},{7,8},{8,9},{9,10},{10,1... | collective-permute-start | bytes 6152 | tf_op jit(solution)/shard_map/ppermute | solution.py:14
  172.1 27.9 %collective-permute-start.10 = (f32[8,1,16,256]{3,2,1,0:T(8,128)}, f32[8,1,16,256]{3,2,1,0:T(8,128)}, u32[]{:S(2)}, u32[]{:S(2)}) collective-permute-start(f32[8,1,16,256]{3,2,1,0:T(8,128)} %get-tuple-element.43), channel_id=1, source_target_pairs={{16,0},{32,16},{48,32},{64,48},{80,64},{96,80},{112,96},{128,112},... | collective-permute-start | bytes 393224 | tf_op jit(solution)/shard_map/ppermute | solution.py:27
  173.4 26.6 %collective-permute-start.11 = (f32[8,1,16,256]{3,2,1,0:T(8,128)}, f32[8,1,16,256]{3,2,1,0:T(8,128)}, u32[]{:S(2)}, u32[]{:S(2)}) collective-permute-start(f32[8,1,16,256]{3,2,1,0:T(8,128)} %get-tuple-element.42), channel_id=1, source_target_pairs={{0,16},{16,32},{32,48},{48,64},{64,80},{80,96},{96,112},{112,128},... | collective-permute-start | bytes 393224 | tf_op jit(solution)/shard_map/ppermute | solution.py:25
  200.0 6.9 %copy-start.21 = (f32[4,8,128]{2,1,0:T(8,128)S(1)}, f32[4,8,128]{2,1,0:T(8,128)}, u32[]{:S(2)}) copy-start(f32[4,8,128]{2,1,0:T(8,128)} %copy-done.20) | copy-start | bytes 49156
  200.0 6.9 %slice-start.1 = ((f32[4,8,128]{2,1,0:T(8,128)}), f32[3,8,128]{2,1,0:T(8,128)S(1)}, s32[]{:S(2)}) async-start(f32[4,8,128]{2,1,0:T(8,128)} %copy-done.20), calls=%async_computation.1 | async-start | bytes 24576 | tf_op jit(solution)/shard_map/slice | solution.py:36
  200.0 6.9 %copy-start.23 = (f32[4,8,128]{2,1,0:T(8,128)S(1)}, f32[4,8,128]{2,1,0:T(8,128)}, u32[]{:S(2)}) copy-start(f32[4,8,128]{2,1,0:T(8,128)} %slice_reduce_fusion) | copy-start | bytes 49156
  200.0 6.9 %copy-start.33 = (f32[4,8,128]{2,1,0:T(8,128)S(1)}, f32[4,8,128]{2,1,0:T(8,128)}, u32[]{:S(2)}) copy-start(f32[4,8,128]{2,1,0:T(8,128)} %reduce_sum.69) | copy-start | bytes 49156
  200.0 8.5 %copy-start.6 = (f32[8,16,256]{2,1,0:T(8,128)S(1)}, f32[8,16,256]{2,1,0:T(8,128)}, u32[]{:S(2)}) copy-start(f32[8,16,256]{2,1,0:T(8,128)} %get-tuple-element.28) | copy-start | bytes 393220
  200.0 8.5 %copy-start.12 = (f32[8,16,256]{2,1,0:T(8,128)S(1)}, f32[8,16,256]{2,1,0:T(8,128)}, u32[]{:S(2)}) copy-start(f32[8,16,256]{2,1,0:T(8,128)} %copy-done.11) | copy-start | bytes 393220
  200.0 8.5 %copy-start.15 = (f32[8,16,256]{2,1,0:T(8,128)S(1)}, f32[8,16,256]{2,1,0:T(8,128)}, u32[]{:S(2)}) copy-start(f32[8,16,256]{2,1,0:T(8,128)} %copy-done.14) | copy-start | bytes 393220
  200.0 8.5 %copy-start.18 = (f32[8,16,256]{2,1,0:T(8,128)S(1)}, f32[8,16,256]{2,1,0:T(8,128)}, u32[]{:S(2)}) copy-start(f32[8,16,256]{2,1,0:T(8,128)} %copy-done.17) | copy-start | bytes 393220
  201.2 7.0 %collective-permute-start.12 = (f32[8,10,1,256]{3,0,2,1:T(8,128)S(1)}, f32[8,10,1,256]{3,0,2,1:T(8,128)S(1)}, u32[]{:S(2)}, u32[]{:S(2)}) collective-permute-start(f32[8,10,1,256]{3,0,2,1:T(8,128)S(1)} %copy.442), channel_id=1, source_target_pairs={{1,0},{2,1},{3,2},{4,3},{5,4},{6,5},{7,6},{8,7},{9,8},{10,9},{11,1... | collective-permute-start | bytes 245768 | tf_op jit(solution)/shard_map/ppermute | solution.py:27
  204.3 4.1 collective-permute-start.13
  237.0 31.6 %copy-start.10 = (f32[8,4,8,128]{3,2,1,0:T(8,128)S(1)}, f32[8,4,8,128]{3,2,1,0:T(8,128)}, u32[]{:S(2)}) copy-start(f32[8,4,8,128]{3,2,1,0:T(8,128)} %copy.447) | copy-start | bytes 393220
  237.0 31.6 %copy-start.22 = (f32[4,8,128]{2,1,0:T(8,128)S(1)}, f32[4,8,128]{2,1,0:T(8,128)}, u32[]{:S(2)}) copy-start(f32[4,8,128]{2,1,0:T(8,128)} %copy-done.20) | copy-start | bytes 49156
  237.0 31.6 %copy-start.24 = (f32[4,8,128]{2,1,0:T(8,128)S(1)}, f32[4,8,128]{2,1,0:T(8,128)}, u32[]{:S(2)}) copy-start(f32[4,8,128]{2,1,0:T(8,128)} %slice_reduce_fusion) | copy-start | bytes 49156
  237.0 31.6 %copy-start.29 = (f32[4,8,128]{2,1,0:T(8,128)S(1)}, f32[4,8,128]{2,1,0:T(8,128)}, u32[]{:S(2)}) copy-start(f32[4,8,128]{2,1,0:T(8,128)} %get-tuple-element.24) | copy-start | bytes 49156
  237.0 31.6 %copy-start.30 = (f32[4,8,128]{2,1,0:T(8,128)S(1)}, f32[4,8,128]{2,1,0:T(8,128)}, u32[]{:S(2)}) copy-start(f32[4,8,128]{2,1,0:T(8,128)} %get-tuple-element.25) | copy-start | bytes 49156
  237.0 31.6 %copy-start.31 = (f32[4,8,128]{2,1,0:T(8,128)S(1)}, f32[4,8,128]{2,1,0:T(8,128)}, u32[]{:S(2)}) copy-start(f32[4,8,128]{2,1,0:T(8,128)} %get-tuple-element.62) | copy-start | bytes 49156
  237.1 31.6 %copy-start.32 = (f32[4,8,128]{2,1,0:T(8,128)S(1)}, f32[4,8,128]{2,1,0:T(8,128)}, u32[]{:S(2)}) copy-start(f32[4,8,128]{2,1,0:T(8,128)} %get-tuple-element.63) | copy-start | bytes 49156
  238.1 5.3 %collective-permute-start.16 = (f32[8,1,8,128]{3,2,1,0:T(8,128)S(1)}, f32[8,1,8,128]{3,2,1,0:T(8,128)S(1)}, u32[]{:S(2)}, u32[]{:S(2)}) collective-permute-start(f32[8,1,8,128]{3,2,1,0:T(8,128)S(1)} %get-tuple-element.59), channel_id=1, source_target_pairs={{16,0},{32,16},{48,32},{64,48},{80,64},{96,80},{112,96},{128,112},... | collective-permute-start | bytes 98312 | tf_op jit(solution)/shard_map/ppermute | solution.py:27
  239.4 5.0 %collective-permute-start.17 = (f32[8,1,8,128]{3,2,1,0:T(8,128)S(1)}, f32[8,1,8,128]{3,2,1,0:T(8,128)S(1)}, u32[]{:S(2)}, u32[]{:S(2)}) collective-permute-start(f32[8,1,8,128]{3,2,1,0:T(8,128)S(1)} %get-tuple-element.58), channel_id=1, source_target_pairs={{0,16},{16,32},{32,48},{48,64},{64,80},{80,96},{96,112},{112,128},... | collective-permute-start | bytes 98312 | tf_op jit(solution)/shard_map/ppermute | solution.py:25
  244.4 7.3 %collective-permute-start.18 = (f32[8,6,1,128]{3,2,1,0:T(1,128)S(1)}, f32[8,6,1,128]{3,2,1,0:T(1,128)S(1)}, u32[]{:S(2)}, u32[]{:S(2)}) collective-permute-start(f32[8,6,1,128]{3,2,1,0:T(1,128)S(1)} %get-tuple-element.52), channel_id=1, source_target_pairs={{1,0},{2,1},{3,2},{4,3},{5,4},{6,5},{7,6},{8,7},{9,8},{10,9},{11,1... | collective-permute-start | bytes 73736 | tf_op jit(solution)/shard_map/ppermute | solution.py:27
  247.4 5.3 %collective-permute-start.19 = (f32[8,6,1,128]{3,2,1,0:T(1,128)S(1)}, f32[8,6,1,128]{3,2,1,0:T(1,128)S(1)}, u32[]{:S(2)}, u32[]{:S(2)}) collective-permute-start(f32[8,6,1,128]{3,2,1,0:T(1,128)S(1)} %get-tuple-element.53), channel_id=1, source_target_pairs={{0,1},{1,2},{2,3},{3,4},{4,5},{5,6},{6,7},{7,8},{8,9},{9,10},{10,1... | collective-permute-start | bytes 73736 | tf_op jit(solution)/shard_map/ppermute | solution.py:25
  253.8 5.9 %collective-permute-start.20 = (f32[8,1,8,128]{3,2,1,0:T(8,128)S(1)}, f32[8,1,8,128]{3,2,1,0:T(8,128)S(1)}, u32[]{:S(2)}, u32[]{:S(2)}) collective-permute-start(f32[8,1,8,128]{3,2,1,0:T(8,128)S(1)} %get-tuple-element.57), channel_id=1, source_target_pairs={{16,0},{32,16},{48,32},{64,48},{80,64},{96,80},{112,96},{128,112},... | collective-permute-start | bytes 98312 | tf_op jit(solution)/shard_map/ppermute | solution.py:27
  255.1 5.6 %collective-permute-start.21 = (f32[8,1,8,128]{3,2,1,0:T(8,128)S(1)}, f32[8,1,8,128]{3,2,1,0:T(8,128)S(1)}, u32[]{:S(2)}, u32[]{:S(2)}) collective-permute-start(f32[8,1,8,128]{3,2,1,0:T(8,128)S(1)} %get-tuple-element.56), channel_id=1, source_target_pairs={{0,16},{16,32},{32,48},{48,64},{64,80},{80,96},{96,112},{112,128},... | collective-permute-start | bytes 98312 | tf_op jit(solution)/shard_map/ppermute | solution.py:25
  260.7 7.0 %collective-permute-start.22 = (f32[8,6,1,128]{3,2,1,0:T(1,128)S(1)}, f32[8,6,1,128]{3,2,1,0:T(1,128)S(1)}, u32[]{:S(2)}, u32[]{:S(2)}) collective-permute-start(f32[8,6,1,128]{3,2,1,0:T(1,128)S(1)} %get-tuple-element.50), channel_id=1, source_target_pairs={{1,0},{2,1},{3,2},{4,3},{5,4},{6,5},{7,6},{8,7},{9,8},{10,9},{11,1... | collective-permute-start | bytes 73736 | tf_op jit(solution)/shard_map/ppermute | solution.py:27
  262.6 6.0 %collective-permute-start.23 = (f32[8,6,1,128]{3,2,1,0:T(1,128)S(1)}, f32[8,6,1,128]{3,2,1,0:T(1,128)S(1)}, u32[]{:S(2)}, u32[]{:S(2)}) collective-permute-start(f32[8,6,1,128]{3,2,1,0:T(1,128)S(1)} %get-tuple-element.51), channel_id=1, source_target_pairs={{0,1},{1,2},{2,3},{3,4},{4,5},{5,6},{6,7},{7,8},{8,9},{9,10},{10,1... | collective-permute-start | bytes 73736 | tf_op jit(solution)/shard_map/ppermute | solution.py:25
  268.8 5.9 %collective-permute-start.24 = (f32[8,1,8,128]{3,2,1,0:T(8,128)S(1)}, f32[8,1,8,128]{3,2,1,0:T(8,128)S(1)}, u32[]{:S(2)}, u32[]{:S(2)}) collective-permute-start(f32[8,1,8,128]{3,2,1,0:T(8,128)S(1)} %get-tuple-element.55), channel_id=1, source_target_pairs={{16,0},{32,16},{48,32},{64,48},{80,64},{96,80},{112,96},{128,112},... | collective-permute-start | bytes 98312 | tf_op jit(solution)/shard_map/ppermute | solution.py:27
  270.1 5.6 %collective-permute-start.25 = (f32[8,1,8,128]{3,2,1,0:T(8,128)S(1)}, f32[8,1,8,128]{3,2,1,0:T(8,128)S(1)}, u32[]{:S(2)}, u32[]{:S(2)}) collective-permute-start(f32[8,1,8,128]{3,2,1,0:T(8,128)S(1)} %get-tuple-element.54), channel_id=1, source_target_pairs={{0,16},{16,32},{32,48},{48,64},{64,80},{80,96},{96,112},{112,128},... | collective-permute-start | bytes 98312 | tf_op jit(solution)/shard_map/ppermute | solution.py:25
  275.8 7.0 %collective-permute-start.26 = (f32[8,6,1,128]{3,2,1,0:T(1,128)S(1)}, f32[8,6,1,128]{3,2,1,0:T(1,128)S(1)}, u32[]{:S(2)}, u32[]{:S(2)}) collective-permute-start(f32[8,6,1,128]{3,2,1,0:T(1,128)S(1)} %get-tuple-element.48), channel_id=1, source_target_pairs={{1,0},{2,1},{3,2},{4,3},{5,4},{6,5},{7,6},{8,7},{9,8},{10,9},{11,1... | collective-permute-start | bytes 73736 | tf_op jit(solution)/shard_map/ppermute | solution.py:27
  277.7 6.0 %collective-permute-start.27 = (f32[8,6,1,128]{3,2,1,0:T(1,128)S(1)}, f32[8,6,1,128]{3,2,1,0:T(1,128)S(1)}, u32[]{:S(2)}, u32[]{:S(2)}) collective-permute-start(f32[8,6,1,128]{3,2,1,0:T(1,128)S(1)} %get-tuple-element.49), channel_id=1, source_target_pairs={{0,1},{1,2},{2,3},{3,4},{4,5},{5,6},{6,7},{7,8},{8,9},{9,10},{10,1... | collective-permute-start | bytes 73736 | tf_op jit(solution)/shard_map/ppermute | solution.py:25
  306.5 16.7 %copy-start.7 = (f32[8,16,256]{2,1,0:T(8,128)S(1)}, f32[8,16,256]{2,1,0:T(8,128)}, u32[]{:S(2)}) copy-start(f32[8,16,256]{2,1,0:T(8,128)} %get-tuple-element.28) | copy-start | bytes 393220
  306.6 16.7 %copy-start.9 = (f32[8,16,256]{2,1,0:T(8,128)S(1)}, f32[8,16,256]{2,1,0:T(8,128)}, u32[]{:S(2)}) copy-start(f32[8,16,256]{2,1,0:T(8,128)} %copy-done.8) | copy-start | bytes 393220
  306.6 16.7 %copy-start.13 = (f32[8,16,256]{2,1,0:T(8,128)S(1)}, f32[8,16,256]{2,1,0:T(8,128)}, u32[]{:S(2)}) copy-start(f32[8,16,256]{2,1,0:T(8,128)} %copy-done.11) | copy-start | bytes 393220
  306.6 16.7 %copy-start.16 = (f32[8,16,256]{2,1,0:T(8,128)S(1)}, f32[8,16,256]{2,1,0:T(8,128)}, u32[]{:S(2)}) copy-start(f32[8,16,256]{2,1,0:T(8,128)} %copy-done.14) | copy-start | bytes 393220
  306.6 16.7 %copy-start.19 = (f32[8,16,256]{2,1,0:T(8,128)S(1)}, f32[8,16,256]{2,1,0:T(8,128)}, u32[]{:S(2)}) copy-start(f32[8,16,256]{2,1,0:T(8,128)} %copy-done.17) | copy-start | bytes 393220
  306.6 6.5 %collective-permute-start.28 = (f32[8,1,16,256]{3,2,1,0:T(8,128)S(1)}, f32[8,1,16,256]{3,2,1,0:T(8,128)S(1)}, u32[]{:S(2)}, u32[]{:S(2)}) collective-permute-start(f32[8,1,16,256]{3,2,1,0:T(8,128)S(1)} %get-tuple-element.41), channel_id=1, source_target_pairs={{16,0},{32,16},{48,32},{64,48},{80,64},{96,80},{112,96},{128,112},... | collective-permute-start | bytes 393224 | tf_op jit(solution)/shard_map/ppermute | solution.py:27
  308.1 6.5 %collective-permute-start.29 = (f32[8,1,16,256]{3,2,1,0:T(8,128)S(1)}, f32[8,1,16,256]{3,2,1,0:T(8,128)S(1)}, u32[]{:S(2)}, u32[]{:S(2)}) collective-permute-start(f32[8,1,16,256]{3,2,1,0:T(8,128)S(1)} %get-tuple-element.40), channel_id=1, source_target_pairs={{0,16},{16,32},{32,48},{48,64},{64,80},{80,96},{96,112},{112,128},... | collective-permute-start | bytes 393224 | tf_op jit(solution)/shard_map/ppermute | solution.py:25
  314.7 7.2 %collective-permute-start.30 = (f32[8,10,1,256]{3,0,2,1:T(8,128)S(1)}, f32[8,10,1,256]{3,0,2,1:T(8,128)S(1)}, u32[]{:S(2)}, u32[]{:S(2)}) collective-permute-start(f32[8,10,1,256]{3,0,2,1:T(8,128)S(1)} %copy.453), channel_id=1, source_target_pairs={{1,0},{2,1},{3,2},{4,3},{5,4},{6,5},{7,6},{8,7},{9,8},{10,9},{11,1... | collective-permute-start | bytes 245768 | tf_op jit(solution)/shard_map/ppermute | solution.py:27
  316.7 6.5 %collective-permute-start.31 = (f32[8,10,1,256]{3,0,2,1:T(8,128)S(1)}, f32[8,10,1,256]{3,0,2,1:T(8,128)S(1)}, u32[]{:S(2)}, u32[]{:S(2)}) collective-permute-start(f32[8,10,1,256]{3,0,2,1:T(8,128)S(1)} %copy.455), channel_id=1, source_target_pairs={{0,1},{1,2},{2,3},{3,4},{4,5},{5,6},{6,7},{7,8},{8,9},{9,10},{10,1... | collective-permute-start | bytes 245768 | tf_op jit(solution)/shard_map/ppermute | solution.py:25
  (5 other events, 10.8 us)
where the time goes:
time: 429 us; the launch traced here: 427 us
  blocking collectives  176 us (41%)
  starting transfers between devices  98.6 us (23%)
  local copies, waits for them, and re-layouts  80.4 us (19%)
  other arithmetic  57.3 us (13%)
  waiting for transfers between devices  9.35 us (2%)
    psum x1, blocking collectives, per_device(): gram = lax.psum(local_gram, ('gx', 'gy'))  93.9 us
    psum x1, blocking collectives, rayleigh_sums(): lax.psum((jnp.sum(vectors * applied, axis=(1, 2, 3)), jnp.sum(vectors * (...  82.2 us
    ppermute x14, starting transfers between devices, with_halo(): lax.ppermute(tail, axis, [(i, (i + 1) % count) for i in range(ends)])  59 us
    ppermute x14, starting transfers between devices, with_halo(): lax.ppermute(head, axis, [((i + 1) % count, i) for i in range(ends)])  26.2 us
    ppermute x4, starting transfers between devices, shifted(): return lax.ppermute(shard, axis, pairs)  13.3 us
    reduce_sum x1, other arithmetic, restrict(): field.reshape(kk, sx // 2, 2, sy // 2, 2, sz // 2, 2).sum(axis=(2, 4, 6))  13.1 us
    reshape x1, local copies, waits for them, and re-layouts, prolong(): jnp.broadcast_to(field[:, :, None, :, None, :, None], (kk, sx, 2, sy, 2,...  10.6 us
    reshape x1, local copies, waits for them, and re-layouts, coarse_weights(): dsum = degree.reshape(shape).sum(axis=(1, 3, 5))  10.5 us
  transfers between devices with their start and end apart: 32, of which 10 were waited for; matrix products, arithmetic and copies ran while one was open for 17% of the time, Pallas kernels for 0%

commit v1 on v0

--- a/solution.py
+++ b/solution.py
@@ -76,11 +76,14 @@
 
 def rayleigh_sums(vectors, applied, degree):
     return lax.psum(
-        (
-            jnp.sum(vectors * applied, axis=(1, 2, 3)),
-            jnp.sum(vectors * (degree[None] * vectors), axis=(1, 2, 3)),
+        lax.psum(
+            (
+                jnp.sum(vectors * applied, axis=(1, 2, 3)),
+                jnp.sum(vectors * (degree[None] * vectors), axis=(1, 2, 3)),
+            ),
+            "gx",
         ),
-        ("gx", "gy"),
+        "gy",
     )
 
 

time: 429 us -> 411 us (0.958)
  blocking collectives: 176 us -> 159 us
    psum x1, blocking collectives: 82.2 us -> 33.1 us  [rayleigh_sums(): lax.psum((jnp.sum(vectors * applied, axis=(1, 2, 3)), jnp.sum(vectors * (...]
    psum x0 -> x1, blocking collectives: none -> 34 us  [rayleigh_sums(): lax.psum(lax.psum((jnp.sum(vectors * applied, axis=(1, 2, 3)), jnp.sum(ve...]
where the time goes in v1:
time: 411 us; the launch traced here: 409 us
  blocking collectives  159 us (39%)
  starting transfers between devices  97.2 us (24%)
  local copies, waits for them, and re-layouts  80.5 us (20%)
  other arithmetic  57.4 us (14%)
  waiting for transfers between devices  9.34 us (2%)
    psum x1, blocking collectives, per_device(): gram = lax.psum(local_gram, ('gx', 'gy'))  92.2 us
    ppermute x14, starting transfers between devices, with_halo(): lax.ppermute(tail, axis, [(i, (i + 1) % count) for i in range(ends)])  58.6 us
    psum x1, blocking collectives, rayleigh_sums(): lax.psum(lax.psum((jnp.sum(vectors * applied, axis=(1, 2, 3)), jnp.sum(ve...  34 us
    psum x1, blocking collectives, rayleigh_sums(): lax.psum((jnp.sum(vectors * applied, axis=(1, 2, 3)), jnp.sum(vectors * (...  33.1 us
    ppermute x14, starting transfers between devices, with_halo(): lax.ppermute(head, axis, [((i + 1) % count, i) for i in range(ends)])  26.4 us
    reduce_sum x1, other arithmetic, restrict(): field.reshape(kk, sx // 2, 2, sy // 2, 2, sz // 2, 2).sum(axis=(2, 4, 6))  13.1 us
    ppermute x4, starting transfers between devices, shifted(): return lax.ppermute(shard, axis, pairs)  12.2 us
    reshape x1, local copies, waits for them, and re-layouts, prolong(): jnp.broadcast_to(field[:, :, None, :, None, :, None], (kk, sx, 2, sy, 2,...  10.6 us
  transfers between devices with their start and end apart: 32, of which 10 were waited for; matrix products, arithmetic and copies ran while one was open for 17% of the time, Pallas kernels for 0%

profile of v1, /device:TPU:1, one launch (start us, length us, event | category | flops | bytes accessed | tf_op | source)
XLA Modules:
  0.0 409.5 jit_solution(4294703556194932448)
XLA Ops:
  1.7 3.9 collective-permute-start
  6.6 4.4 %collective-permute-start.1 = (f32[8,1,256]{2,1,0:T(1,128)S(1)}, f32[8,1,256]{2,1,0:T(1,128)S(1)}, u32[]{:S(2)}, u32[]{:S(2)}) collective-permute-start(f32[8,1,256]{2,1,0:T(1,128)S(1)} %slice.374), channel_id=1, source_target_pairs={{0,1},{1,2},{2,3},{3,4},{4,5},{5,6},{6,7},{7,8},{8,9},{9,10},{10,1... | collective-permute-start | bytes 24584 | tf_op jit(solution)/shard_map/ppermute | solution.py:14
  12.0 3.1 collective-permute-start.3
  15.2 1.3 collective-permute-start.2
  16.5 9.8 %reshape.74 = f32[4,2,8,2,128,2]{5,4,3,2,1,0:T(8,128)} reshape(f32[8,16,256]{2,1,0:T(8,128)S(1)} %broadcast_select_fusion.2) | data formatting | bytes 262144 | tf_op jit(solution)/shard_map/reshape | solution.py:93
  26.6 1.9 collective-permute-start.4
  28.6 3.6 collective-permute-start.5
  33.8 2.1 fusion
  35.9 33.1 %all-reduce.10 = (f32[8]{0:T(128)S(1)}, f32[8]{0:T(128)S(1)}) all-reduce(f32[8]{0:T(128)S(1)} %get-tuple-element.19, f32[8]{0:T(128)S(1)} %get-tuple-element.18), channel_id=1, replica_groups=mesh['gx'=16,'gy'=16] {'gx'}, use_global_device_ids=true, to_apply=%region_1.2 | all-reduce | flops 16 | bytes 128 | tf_op jit(solution)/shard_map/psum | solution.py:79
  69.0 34.0 %all-reduce.9 = (f32[8]{0:T(128)S(1)}, f32[8]{0:T(128)S(1)}) all-reduce(f32[8]{0:T(128)S(1)} %get-tuple-element.22, f32[8]{0:T(128)S(1)} %get-tuple-element.23), channel_id=1, replica_groups=mesh['gx'=16,'gy'=16] {'gy'}, use_global_device_ids=true, to_apply=%region_2.3 | all-reduce | flops 16 | bytes 128 | tf_op jit(solution)/shard_map/psum | solution.py:78
  103.0 1.7 multiply_divide_fusion
  105.5 1.3 collective-permute-start.6
  106.8 4.6 %collective-permute-start.7 = (f32[8,1,16,256]{3,2,1,0:T(8,128)}, f32[8,1,16,256]{3,2,1,0:T(8,128)}, u32[]{:S(2)}, u32[]{:S(2)}) collective-permute-start(f32[8,1,16,256]{3,2,1,0:T(8,128)} %get-tuple-element.46), channel_id=1, source_target_pairs={{0,16},{16,32},{32,48},{48,64},{64,80},{80,96},{96,112},{112,128},... | collective-permute-start | bytes 393224 | tf_op jit(solution)/shard_map/ppermute | solution.py:25
  111.4 2.8 slice_reduce_fusion.2
  115.4 1.9 collective-permute-start.14
  117.3 9.8 %reshape.75 = f32[4,2,8,2,128,2]{5,4,3,2,1,0:T(8,128)} reshape(f32[8,16,256]{2,1,0:T(8,128)S(1)} %broadcast_select_fusion.1) | data formatting | bytes 262144 | tf_op jit(solution)/shard_map/reshape | solution.py:94
  127.1 1.0 pad_maximum_fusion.62
  128.1 2.6 collective-permute-start.8
  130.8 2.9 collective-permute-start.9
  133.7 2.8 slice_reduce_fusion.1
  137.1 2.0 collective-permute-start.15
  139.2 9.8 %reshape.76 = f32[4,2,8,2,128,2]{5,4,3,2,1,0:T(8,128)} reshape(f32[8,16,256]{2,1,0:T(8,128)S(1)} %broadcast_select_fusion) | data formatting | bytes 262144 | tf_op jit(solution)/shard_map/reshape | solution.py:95
  149.2 5.3 %fusion.13 = f32[8,8,16,256]{3,2,1,0:T(8,128)S(1)} fusion(f32[8,8,16,256]{3,2,1,0:T(8,128)} %copy-done.1, f32[8,8,16,256]{3,2,1,0:T(8,128)S(1)} %get-tuple-element.29, f32[8,10,1,256]{3,2,1,0:T(1,128)S(1)} %copy.441, f32[8,1,16,256]{3,2,1,0:T(8,128)} %copy-done.25, f32[8,1,16,256]{3,2,1,0:T(8,128)} %collective-permute-done.7, ...), kind=kLoop, calls=%fused_computation.28 | loop fusion | flops 6553600 | bytes 4489216 | tf_op jit(solution)/shard_map/add | solution.py:72
  155.2 1.3 collective-permute-start.10
  156.5 4.6 %collective-permute-start.11 = (f32[8,1,16,256]{3,2,1,0:T(8,128)}, f32[8,1,16,256]{3,2,1,0:T(8,128)}, u32[]{:S(2)}, u32[]{:S(2)}) collective-permute-start(f32[8,1,16,256]{3,2,1,0:T(8,128)} %get-tuple-element.44), channel_id=1, source_target_pairs={{0,16},{16,32},{32,48},{48,64},{64,80},{80,96},{96,112},{112,128},... | collective-permute-start | bytes 393224 | tf_op jit(solution)/shard_map/ppermute | solution.py:25
  161.2 6.8 %slice_reduce_fusion = f32[4,8,128]{2,1,0:T(8,128)} fusion(f32[4,2,8,2,128,2]{5,4,3,2,1,0:T(8,128)} %reshape.76), kind=kLoop, calls=%fused_computation | loop fusion | flops 12288 | bytes 81920 | tf_op jit(solution)/shard_map/reduce_sum | solution.py:95
  167.9 10.5 %reshape.77 = f32[4,2,8,2,128,2]{5,4,3,2,1,0:T(8,128)} reshape(f32[8,16,256]{2,1,0:T(8,128)} %copy-done.8) | data formatting | bytes 262144 | tf_op jit(solution)/shard_map/reshape | solution.py:96
  178.5 4.6 %reduce_sum.69 = f32[4,8,128]{2,1,0:T(8,128)} reduce(f32[4,2,8,2,128,2]{5,4,3,2,1,0:T(8,128)} %reshape.77, f32[]{:T(128)} %constant.65.clone.1), dimensions={1,3,5}, to_apply=%region_10.11 | reduce | flops 28672 | bytes 147460 | tf_op jit(solution)/shard_map/reduce_sum | solution.py:96
  183.1 1.2 pad_maximum_fusion.59
  184.3 3.5 collective-permute-start.12
  187.9 2.0 collective-permute-start.13
  190.0 1.4 multiply_add_fusion
  191.6 2.8 fusion.19
  194.4 9.8 %copy.446 = f32[8,8,16,256]{0,3,2,1:T(8,128)} copy(f32[8,8,16,256]{3,2,1,0:T(8,128)} %fusion.19) | data formatting | bytes 2097152 | tf_op jit(solution)/shard_map/sub | solution.py:131
  204.3 13.1 %reduce_sum.65 = f32[8,4,8,128]{0,3,2,1:T(8,128)} reduce(f32[8,4,2,8,2,128,2]{0,6,5,4,3,2,1:T(2,128)} %bitcast.30, f32[]{:T(128)} %constant.65.clone.1), dimensions={2,4,6}, to_apply=%region_6.7 | reduce | flops 229376 | bytes 1179652 | tf_op jit(solution)/shard_map/reduce_sum | solution.py:102
  217.4 2.8 copy.447
  221.3 1.3 collective-permute-start.16
  222.6 4.0 collective-permute-start.17
  227.6 3.4 collective-permute-start.18
  231.0 3.8 collective-permute-start.19
  235.8 1.1 fusion.68
  236.9 1.3 collective-permute-start.20
  238.2 4.6 %collective-permute-start.21 = (f32[8,1,8,128]{3,2,1,0:T(8,128)S(1)}, f32[8,1,8,128]{3,2,1,0:T(8,128)S(1)}, u32[]{:S(2)}, u32[]{:S(2)}) collective-permute-start(f32[8,1,8,128]{3,2,1,0:T(8,128)S(1)} %get-tuple-element.58), channel_id=1, source_target_pairs={{0,16},{16,32},{32,48},{48,64},{64,80},{80,96},{96,112},{112,128},... | collective-permute-start | bytes 98312 | tf_op jit(solution)/shard_map/ppermute | solution.py:25
  243.9 1.9 collective-permute-start.22
  245.8 5.1 %collective-permute-start.23 = (f32[8,6,1,128]{3,2,1,0:T(1,128)S(1)}, f32[8,6,1,128]{3,2,1,0:T(1,128)S(1)}, u32[]{:S(2)}, u32[]{:S(2)}) collective-permute-start(f32[8,6,1,128]{3,2,1,0:T(1,128)S(1)} %get-tuple-element.53), channel_id=1, source_target_pairs={{0,1},{1,2},{2,3},{3,4},{4,5},{5,6},{6,7},{7,8},{8,9},{9,10},{10,1... | collective-permute-start | bytes 73736 | tf_op jit(solution)/shard_map/ppermute | solution.py:25
  252.0 1.3 collective-permute-start.24
  253.3 4.6 %collective-permute-start.25 = (f32[8,1,8,128]{3,2,1,0:T(8,128)S(1)}, f32[8,1,8,128]{3,2,1,0:T(8,128)S(1)}, u32[]{:S(2)}, u32[]{:S(2)}) collective-permute-start(f32[8,1,8,128]{3,2,1,0:T(8,128)S(1)} %get-tuple-element.56), channel_id=1, source_target_pairs={{0,16},{16,32},{32,48},{48,64},{64,80},{80,96},{96,112},{112,128},... | collective-permute-start | bytes 98312 | tf_op jit(solution)/shard_map/ppermute | solution.py:25
  258.9 1.9 collective-permute-start.26
  260.8 5.1 %collective-permute-start.27 = (f32[8,6,1,128]{3,2,1,0:T(1,128)S(1)}, f32[8,6,1,128]{3,2,1,0:T(1,128)S(1)}, u32[]{:S(2)}, u32[]{:S(2)}) collective-permute-start(f32[8,6,1,128]{3,2,1,0:T(1,128)S(1)} %get-tuple-element.51), channel_id=1, source_target_pairs={{0,1},{1,2},{2,3},{3,4},{4,5},{5,6},{6,7},{7,8},{8,9},{9,10},{10,1... | collective-permute-start | bytes 73736 | tf_op jit(solution)/shard_map/ppermute | solution.py:25
  267.7 2.9 copy.451
  270.5 7.1 %broadcast_in_dim.30 = f32[8,4,2,8,2,128,2]{0,6,5,4,3,2,1:T(2,128)} broadcast(f32[8,4,8,128]{0,3,2,1:T(8,128)} %copy.451), dimensions={0,1,3,5} | broadcast | bytes 1179648 | tf_op jit(solution)/shard_map/broadcast_in_dim | solution.py:107
  277.7 10.6 %copy.452 = f32[8,8,16,256]{3,2,1,0:T(8,128)} copy(f32[8,8,16,256]{0,3,2,1:T(8,128)} %bitcast.31) | data formatting | bytes 2097152 | tf_op jit(solution)/shard_map/reshape | solution.py:107
  288.3 1.4 add.267
  289.8 1.4 collective-permute-start.28
  291.2 4.6 %collective-permute-start.29 = (f32[8,1,16,256]{3,2,1,0:T(8,128)S(1)}, f32[8,1,16,256]{3,2,1,0:T(8,128)S(1)}, u32[]{:S(2)}, u32[]{:S(2)}) collective-permute-start(f32[8,1,16,256]{3,2,1,0:T(8,128)S(1)} %get-tuple-element.42), channel_id=1, source_target_pairs={{0,16},{16,32},{32,48},{48,64},{64,80},{80,96},{96,112},{112,128},... | collective-permute-start | bytes 393224 | tf_op jit(solution)/shard_map/ppermute | solution.py:25
  296.2 1.5 collective-permute-done.29
  297.9 1.9 collective-permute-start.30
  299.8 5.8 %collective-permute-start.31 = (f32[8,10,1,256]{3,0,2,1:T(8,128)S(1)}, f32[8,10,1,256]{3,0,2,1:T(8,128)S(1)}, u32[]{:S(2)}, u32[]{:S(2)}) collective-permute-start(f32[8,10,1,256]{3,0,2,1:T(8,128)S(1)} %copy.455), channel_id=1, source_target_pairs={{0,1},{1,2},{2,3},{3,4},{4,5},{5,6},{6,7},{7,8},{8,9},{9,10},{10,1... | collective-permute-start | bytes 245768 | tf_op jit(solution)/shard_map/ppermute | solution.py:25
  305.8 1.1 collective-permute-done.31
  307.0 1.6 broadcast_multiply_fusion
  308.6 3.0 convolution_bitcast_fusion
  311.6 92.2 %psum.39 = f32[8,8]{0,1:T(8,128)S(1)} all-reduce(f32[8,8]{0,1:T(8,128)S(1)} %convolution_bitcast_fusion), channel_id=1, replica_groups=mesh['gx'=16,'gy'=16] {'gx','gy'}, use_global_device_ids=true, to_apply=%region_11.12 | all-reduce | flops 64 | bytes 512 | tf_op jit(solution)/shard_map/psum | solution.py:145
  407.2 1.0 fusion.110
  408.2 1.3 copy.462
  (159 shorter events, 20.5 us)
Async XLA Ops:
  1.6 24.6 %copy-start.2 = (f32[8,16,256]{2,1,0:T(8,128)}, f32[8,16,256]{2,1,0:T(8,128)S(1)}, u32[]{:S(2)}) copy-start(f32[8,16,256]{2,1,0:T(8,128)S(1)} %broadcast_select_fusion.2) | copy-start | bytes 393220
  1.7 30.6 %collective-permute-start = (f32[1,16,256]{2,1,0:T(8,128)S(1)}, f32[1,16,256]{2,1,0:T(8,128)S(1)}, u32[]{:S(2)}, u32[]{:S(2)}) collective-permute-start(f32[1,16,256]{2,1,0:T(8,128)S(1)} %slice.372), channel_id=1, source_target_pairs={{0,16},{16,32},{32,48},{48,64},{64,80},{80,96},{96,112},{112,128},... | collective-permute-start | bytes 49160 | tf_op jit(solution)/shard_map/ppermute | solution.py:14
  6.6 25.6 %collective-permute-start.1 = (f32[8,1,256]{2,1,0:T(1,128)S(1)}, f32[8,1,256]{2,1,0:T(1,128)S(1)}, u32[]{:S(2)}, u32[]{:S(2)}) collective-permute-start(f32[8,1,256]{2,1,0:T(1,128)S(1)} %slice.374), channel_id=1, source_target_pairs={{0,1},{1,2},{2,3},{3,4},{4,5},{5,6},{6,7},{7,8},{8,9},{9,10},{10,1... | collective-permute-start | bytes 24584 | tf_op jit(solution)/shard_map/ppermute | solution.py:14
  12.0 14.3 %collective-permute-start.3 = (f32[8,1,16,256]{3,2,1,0:T(8,128)S(1)}, f32[8,1,16,256]{3,2,1,0:T(8,128)S(1)}, u32[]{:S(2)}, u32[]{:S(2)}) collective-permute-start(f32[8,1,16,256]{3,2,1,0:T(8,128)S(1)} %get-tuple-element.49), channel_id=1, source_target_pairs={{0,16},{16,32},{32,48},{48,64},{64,80},{80,96},{96,112},{112,128},... | collective-permute-start | bytes 393224 | tf_op jit(solution)/shard_map/ppermute | solution.py:25
  15.2 11.3 %collective-permute-start.2 = (f32[8,1,16,256]{3,2,1,0:T(8,128)S(1)}, f32[8,1,16,256]{3,2,1,0:T(8,128)S(1)}, u32[]{:S(2)}, u32[]{:S(2)}) collective-permute-start(f32[8,1,16,256]{3,2,1,0:T(8,128)S(1)} %get-tuple-element.48), channel_id=1, source_target_pairs={{16,0},{32,16},{48,32},{64,48},{80,64},{96,80},{112,96},{128,112},... | collective-permute-start | bytes 393224 | tf_op jit(solution)/shard_map/ppermute | solution.py:27
  16.5 9.8 %copy-start.26 = (f32[8,16,256]{2,1,0:T(8,128)S(1)}, f32[8,16,256]{2,1,0:T(8,128)}, u32[]{:S(2)}) copy-start(f32[8,16,256]{2,1,0:T(8,128)} %param.7) | copy-start | bytes 393220
  16.5 9.8 %copy-start = (f32[8,8,16,256]{3,2,1,0:T(8,128)S(1)}, f32[8,8,16,256]{3,2,1,0:T(8,128)}, u32[]{:S(2)}) copy-start(f32[8,8,16,256]{3,2,1,0:T(8,128)} %param.4) | copy-start | bytes 3145732
  26.3 5.9 %slice-start = ((f32[8,16,256]{2,1,0:T(8,128)}), f32[7,16,256]{2,1,0:T(8,128)S(1)}, s32[]{:S(2)}) async-start(f32[8,16,256]{2,1,0:T(8,128)} %copy-done.2), calls=%async_computation | async-start | bytes 229376 | tf_op jit(solution)/shard_map/slice | solution.py:36
  26.3 5.9 %copy-start.27 = (f32[8,16,256]{2,1,0:T(8,128)S(1)}, f32[8,16,256]{2,1,0:T(8,128)}, u32[]{:S(2)}) copy-start(f32[8,16,256]{2,1,0:T(8,128)} %param.5) | copy-start | bytes 393220
  26.4 5.9 %copy-start.28 = (f32[8,16,256]{2,1,0:T(8,128)S(1)}, f32[8,16,256]{2,1,0:T(8,128)}, u32[]{:S(2)}) copy-start(f32[8,16,256]{2,1,0:T(8,128)} %param.6) | copy-start | bytes 393220
  26.5 7.3 %copy-start.3 = (f32[8,16,256]{2,1,0:T(8,128)S(1)}, f32[8,16,256]{2,1,0:T(8,128)}, u32[]{:S(2)}) copy-start(f32[8,16,256]{2,1,0:T(8,128)} %copy-done.2) | copy-start | bytes 393220
  26.6 6.5 %collective-permute-start.4 = (f32[8,10,1,256]{3,0,2,1:T(8,128)S(1)}, f32[8,10,1,256]{3,0,2,1:T(8,128)S(1)}, u32[]{:S(2)}, u32[]{:S(2)}) collective-permute-start(f32[8,10,1,256]{3,0,2,1:T(8,128)S(1)} %copy.466), channel_id=1, source_target_pairs={{1,0},{2,1},{3,2},{4,3},{5,4},{6,5},{7,6},{8,7},{9,8},{10,9},{11,1... | collective-permute-start | bytes 245768 | tf_op jit(solution)/shard_map/ppermute | solution.py:27
  28.6 5.1 %collective-permute-start.5 = (f32[8,10,1,256]{3,0,2,1:T(8,128)S(1)}, f32[8,10,1,256]{3,0,2,1:T(8,128)S(1)}, u32[]{:S(2)}, u32[]{:S(2)}) collective-permute-start(f32[8,10,1,256]{3,0,2,1:T(8,128)S(1)} %copy.467), channel_id=1, source_target_pairs={{0,1},{1,2},{2,3},{3,4},{4,5},{5,6},{6,7},{7,8},{8,9},{9,10},{10,1... | collective-permute-start | bytes 245768 | tf_op jit(solution)/shard_map/ppermute | solution.py:25
  33.1 2.8 copy-start.17
  33.8 69.2 %copy-start.5 = (f32[8,16,256]{2,1,0:T(8,128)S(1)}, f32[8,16,256]{2,1,0:T(8,128)}, u32[]{:S(2)}) copy-start(f32[8,16,256]{2,1,0:T(8,128)} %get-tuple-element.30) | copy-start | bytes 393220
  104.7 22.3 %copy-start.1 = (f32[8,8,16,256]{3,2,1,0:T(8,128)}, f32[8,8,16,256]{3,2,1,0:T(8,128)S(1)}, u32[]{:S(2)}) copy-start(f32[8,8,16,256]{3,2,1,0:T(8,128)S(1)} %get-tuple-element.28) | copy-start | bytes 3145732
  105.5 21.6 %collective-permute-start.6 = (f32[8,1,16,256]{3,2,1,0:T(8,128)}, f32[8,1,16,256]{3,2,1,0:T(8,128)S(1)}, u32[]{:S(2)}, u32[]{:S(2)}) collective-permute-start(f32[8,1,16,256]{3,2,1,0:T(8,128)} %get-tuple-element.47), channel_id=1, source_target_pairs={{16,0},{32,16},{48,32},{64,48},{80,64},{96,80},{112,96},{128,112},... | collective-permute-start | bytes 393224 | tf_op jit(solution)/shard_map/ppermute | solution.py:27
  106.8 20.3 %collective-permute-start.7 = (f32[8,1,16,256]{3,2,1,0:T(8,128)}, f32[8,1,16,256]{3,2,1,0:T(8,128)}, u32[]{:S(2)}, u32[]{:S(2)}) collective-permute-start(f32[8,1,16,256]{3,2,1,0:T(8,128)} %get-tuple-element.46), channel_id=1, source_target_pairs={{0,16},{16,32},{32,48},{48,64},{64,80},{80,96},{96,112},{112,128},... | collective-permute-start | bytes 393224 | tf_op jit(solution)/shard_map/ppermute | solution.py:25
  115.4 74.5 %collective-permute-start.14 = (f32[1,8,128]{2,1,0:T(8,128)}, f32[1,8,128]{2,1,0:T(8,128)}, u32[]{:S(2)}, u32[]{:S(2)}) collective-permute-start(f32[1,8,128]{2,1,0:T(8,128)} %slice.384), channel_id=1, source_target_pairs={{0,16},{16,32},{32,48},{48,64},{64,80},{80,96},{96,112},{112,128},... | collective-permute-start | bytes 12296 | tf_op jit(solution)/shard_map/ppermute | solution.py:14
  127.1 9.5 %copy-start.25 = (f32[8,1,16,256]{3,2,1,0:T(8,128)}, f32[8,1,16,256]{3,2,1,0:T(8,128)S(1)}, u32[]{:S(2)}) copy-start(f32[8,1,16,256]{3,2,1,0:T(8,128)S(1)} %collective-permute-done.6) | copy-start | bytes 393220
  128.1 20.8 %collective-permute-start.8 = (f32[8,10,1,256]{3,0,2,1:T(8,128)S(1)}, f32[8,10,1,256]{3,0,2,1:T(8,128)S(1)}, u32[]{:S(2)}, u32[]{:S(2)}) collective-permute-start(f32[8,10,1,256]{3,0,2,1:T(8,128)S(1)} %copy.438), channel_id=1, source_target_pairs={{1,0},{2,1},{3,2},{4,3},{5,4},{6,5},{7,6},{8,7},{9,8},{10,9},{11,1... | collective-permute-start | bytes 245768 | tf_op jit(solution)/shard_map/ppermute | solution.py:27
  130.8 18.3 %collective-permute-start.9 = (f32[8,10,1,256]{3,0,2,1:T(8,128)S(1)}, f32[8,10,1,256]{3,0,2,1:T(8,128)S(1)}, u32[]{:S(2)}, u32[]{:S(2)}) collective-permute-start(f32[8,10,1,256]{3,0,2,1:T(8,128)S(1)} %copy.440), channel_id=1, source_target_pairs={{0,1},{1,2},{2,3},{3,4},{4,5},{5,6},{6,7},{7,8},{8,9},{9,10},{10,1... | collective-permute-start | bytes 245768 | tf_op jit(solution)/shard_map/ppermute | solution.py:25
  137.1 12.0 %copy-start.4 = (f32[8,16,256]{2,1,0:T(8,128)S(1)}, f32[8,16,256]{2,1,0:T(8,128)}, u32[]{:S(2)}) copy-start(f32[8,16,256]{2,1,0:T(8,128)} %copy-done.2) | copy-start | bytes 393220
  137.1 52.8 %collective-permute-start.15 = (f32[4,1,128]{2,1,0:T(1,128)}, f32[4,1,128]{2,1,0:T(1,128)}, u32[]{:S(2)}, u32[]{:S(2)}) collective-permute-start(f32[4,1,128]{2,1,0:T(1,128)} %slice.387), channel_id=1, source_target_pairs={{0,1},{1,2},{2,3},{3,4},{4,5},{5,6},{6,7},{7,8},{8,9},{9,10},{10,1... | collective-permute-start | bytes 6152 | tf_op jit(solution)/shard_map/ppermute | solution.py:14
  155.2 27.9 %collective-permute-start.10 = (f32[8,1,16,256]{3,2,1,0:T(8,128)}, f32[8,1,16,256]{3,2,1,0:T(8,128)}, u32[]{:S(2)}, u32[]{:S(2)}) collective-permute-start(f32[8,1,16,256]{3,2,1,0:T(8,128)} %get-tuple-element.45), channel_id=1, source_target_pairs={{16,0},{32,16},{48,32},{64,48},{80,64},{96,80},{112,96},{128,112},... | collective-permute-start | bytes 393224 | tf_op jit(solution)/shard_map/ppermute | solution.py:27
  156.5 26.6 %collective-permute-start.11 = (f32[8,1,16,256]{3,2,1,0:T(8,128)}, f32[8,1,16,256]{3,2,1,0:T(8,128)}, u32[]{:S(2)}, u32[]{:S(2)}) collective-permute-start(f32[8,1,16,256]{3,2,1,0:T(8,128)} %get-tuple-element.44), channel_id=1, source_target_pairs={{0,16},{16,32},{32,48},{48,64},{64,80},{80,96},{96,112},{112,128},... | collective-permute-start | bytes 393224 | tf_op jit(solution)/shard_map/ppermute | solution.py:25
  183.1 6.9 %copy-start.21 = (f32[4,8,128]{2,1,0:T(8,128)S(1)}, f32[4,8,128]{2,1,0:T(8,128)}, u32[]{:S(2)}) copy-start(f32[4,8,128]{2,1,0:T(8,128)} %copy-done.20) | copy-start | bytes 49156
  183.1 6.9 %slice-start.1 = ((f32[4,8,128]{2,1,0:T(8,128)}), f32[3,8,128]{2,1,0:T(8,128)S(1)}, s32[]{:S(2)}) async-start(f32[4,8,128]{2,1,0:T(8,128)} %copy-done.20), calls=%async_computation.1 | async-start | bytes 24576 | tf_op jit(solution)/shard_map/slice | solution.py:36
  183.1 6.9 %copy-start.23 = (f32[4,8,128]{2,1,0:T(8,128)S(1)}, f32[4,8,128]{2,1,0:T(8,128)}, u32[]{:S(2)}) copy-start(f32[4,8,128]{2,1,0:T(8,128)} %slice_reduce_fusion) | copy-start | bytes 49156
  183.1 6.9 %copy-start.33 = (f32[4,8,128]{2,1,0:T(8,128)S(1)}, f32[4,8,128]{2,1,0:T(8,128)}, u32[]{:S(2)}) copy-start(f32[4,8,128]{2,1,0:T(8,128)} %reduce_sum.69) | copy-start | bytes 49156
  183.1 8.5 %copy-start.6 = (f32[8,16,256]{2,1,0:T(8,128)S(1)}, f32[8,16,256]{2,1,0:T(8,128)}, u32[]{:S(2)}) copy-start(f32[8,16,256]{2,1,0:T(8,128)} %get-tuple-element.30) | copy-start | bytes 393220
  183.1 8.5 %copy-start.12 = (f32[8,16,256]{2,1,0:T(8,128)S(1)}, f32[8,16,256]{2,1,0:T(8,128)}, u32[]{:S(2)}) copy-start(f32[8,16,256]{2,1,0:T(8,128)} %copy-done.11) | copy-start | bytes 393220
  183.1 8.5 %copy-start.15 = (f32[8,16,256]{2,1,0:T(8,128)S(1)}, f32[8,16,256]{2,1,0:T(8,128)}, u32[]{:S(2)}) copy-start(f32[8,16,256]{2,1,0:T(8,128)} %copy-done.14) | copy-start | bytes 393220
  183.1 8.5 %copy-start.18 = (f32[8,16,256]{2,1,0:T(8,128)S(1)}, f32[8,16,256]{2,1,0:T(8,128)}, u32[]{:S(2)}) copy-start(f32[8,16,256]{2,1,0:T(8,128)} %copy-done.17) | copy-start | bytes 393220
  184.3 7.0 %collective-permute-start.12 = (f32[8,10,1,256]{3,0,2,1:T(8,128)S(1)}, f32[8,10,1,256]{3,0,2,1:T(8,128)S(1)}, u32[]{:S(2)}, u32[]{:S(2)}) collective-permute-start(f32[8,10,1,256]{3,0,2,1:T(8,128)S(1)} %copy.442), channel_id=1, source_target_pairs={{1,0},{2,1},{3,2},{4,3},{5,4},{6,5},{7,6},{8,7},{9,8},{10,9},{11,1... | collective-permute-start | bytes 245768 | tf_op jit(solution)/shard_map/ppermute | solution.py:27
  187.9 3.6 collective-permute-start.13
  220.2 31.6 %copy-start.10 = (f32[8,4,8,128]{3,2,1,0:T(8,128)S(1)}, f32[8,4,8,128]{3,2,1,0:T(8,128)}, u32[]{:S(2)}) copy-start(f32[8,4,8,128]{3,2,1,0:T(8,128)} %copy.447) | copy-start | bytes 393220
  220.2 31.6 %copy-start.22 = (f32[4,8,128]{2,1,0:T(8,128)S(1)}, f32[4,8,128]{2,1,0:T(8,128)}, u32[]{:S(2)}) copy-start(f32[4,8,128]{2,1,0:T(8,128)} %copy-done.20) | copy-start | bytes 49156
  220.2 31.6 %copy-start.24 = (f32[4,8,128]{2,1,0:T(8,128)S(1)}, f32[4,8,128]{2,1,0:T(8,128)}, u32[]{:S(2)}) copy-start(f32[4,8,128]{2,1,0:T(8,128)} %slice_reduce_fusion) | copy-start | bytes 49156
  220.2 31.6 %copy-start.29 = (f32[4,8,128]{2,1,0:T(8,128)S(1)}, f32[4,8,128]{2,1,0:T(8,128)}, u32[]{:S(2)}) copy-start(f32[4,8,128]{2,1,0:T(8,128)} %get-tuple-element.26) | copy-start | bytes 49156
  220.2 31.6 %copy-start.30 = (f32[4,8,128]{2,1,0:T(8,128)S(1)}, f32[4,8,128]{2,1,0:T(8,128)}, u32[]{:S(2)}) copy-start(f32[4,8,128]{2,1,0:T(8,128)} %get-tuple-element.27) | copy-start | bytes 49156
  220.2 31.6 %copy-start.31 = (f32[4,8,128]{2,1,0:T(8,128)S(1)}, f32[4,8,128]{2,1,0:T(8,128)}, u32[]{:S(2)}) copy-start(f32[4,8,128]{2,1,0:T(8,128)} %get-tuple-element.64) | copy-start | bytes 49156
  220.2 31.6 %copy-start.32 = (f32[4,8,128]{2,1,0:T(8,128)S(1)}, f32[4,8,128]{2,1,0:T(8,128)}, u32[]{:S(2)}) copy-start(f32[4,8,128]{2,1,0:T(8,128)} %get-tuple-element.65) | copy-start | bytes 49156
  221.3 5.3 %collective-permute-start.16 = (f32[8,1,8,128]{3,2,1,0:T(8,128)S(1)}, f32[8,1,8,128]{3,2,1,0:T(8,128)S(1)}, u32[]{:S(2)}, u32[]{:S(2)}) collective-permute-start(f32[8,1,8,128]{3,2,1,0:T(8,128)S(1)} %get-tuple-element.61), channel_id=1, source_target_pairs={{16,0},{32,16},{48,32},{64,48},{80,64},{96,80},{112,96},{128,112},... | collective-permute-start | bytes 98312 | tf_op jit(solution)/shard_map/ppermute | solution.py:27
  222.6 5.0 %collective-permute-start.17 = (f32[8,1,8,128]{3,2,1,0:T(8,128)S(1)}, f32[8,1,8,128]{3,2,1,0:T(8,128)S(1)}, u32[]{:S(2)}, u32[]{:S(2)}) collective-permute-start(f32[8,1,8,128]{3,2,1,0:T(8,128)S(1)} %get-tuple-element.60), channel_id=1, source_target_pairs={{0,16},{16,32},{32,48},{48,64},{64,80},{80,96},{96,112},{112,128},... | collective-permute-start | bytes 98312 | tf_op jit(solution)/shard_map/ppermute | solution.py:25
  227.6 7.3 %collective-permute-start.18 = (f32[8,6,1,128]{3,2,1,0:T(1,128)S(1)}, f32[8,6,1,128]{3,2,1,0:T(1,128)S(1)}, u32[]{:S(2)}, u32[]{:S(2)}) collective-permute-start(f32[8,6,1,128]{3,2,1,0:T(1,128)S(1)} %get-tuple-element.54), channel_id=1, source_target_pairs={{1,0},{2,1},{3,2},{4,3},{5,4},{6,5},{7,6},{8,7},{9,8},{10,9},{11,1... | collective-permute-start | bytes 73736 | tf_op jit(solution)/shard_map/ppermute | solution.py:27
  231.0 4.8 %collective-permute-start.19 = (f32[8,6,1,128]{3,2,1,0:T(1,128)S(1)}, f32[8,6,1,128]{3,2,1,0:T(1,128)S(1)}, u32[]{:S(2)}, u32[]{:S(2)}) collective-permute-start(f32[8,6,1,128]{3,2,1,0:T(1,128)S(1)} %get-tuple-element.55), channel_id=1, source_target_pairs={{0,1},{1,2},{2,3},{3,4},{4,5},{5,6},{6,7},{7,8},{8,9},{9,10},{10,1... | collective-permute-start | bytes 73736 | tf_op jit(solution)/shard_map/ppermute | solution.py:25
  236.9 5.9 %collective-permute-start.20 = (f32[8,1,8,128]{3,2,1,0:T(8,128)S(1)}, f32[8,1,8,128]{3,2,1,0:T(8,128)S(1)}, u32[]{:S(2)}, u32[]{:S(2)}) collective-permute-start(f32[8,1,8,128]{3,2,1,0:T(8,128)S(1)} %get-tuple-element.59), channel_id=1, source_target_pairs={{16,0},{32,16},{48,32},{64,48},{80,64},{96,80},{112,96},{128,112},... | collective-permute-start | bytes 98312 | tf_op jit(solution)/shard_map/ppermute | solution.py:27
  238.2 5.6 %collective-permute-start.21 = (f32[8,1,8,128]{3,2,1,0:T(8,128)S(1)}, f32[8,1,8,128]{3,2,1,0:T(8,128)S(1)}, u32[]{:S(2)}, u32[]{:S(2)}) collective-permute-start(f32[8,1,8,128]{3,2,1,0:T(8,128)S(1)} %get-tuple-element.58), channel_id=1, source_target_pairs={{0,16},{16,32},{32,48},{48,64},{64,80},{80,96},{96,112},{112,128},... | collective-permute-start | bytes 98312 | tf_op jit(solution)/shard_map/ppermute | solution.py:25
  243.9 7.0 %collective-permute-start.22 = (f32[8,6,1,128]{3,2,1,0:T(1,128)S(1)}, f32[8,6,1,128]{3,2,1,0:T(1,128)S(1)}, u32[]{:S(2)}, u32[]{:S(2)}) collective-permute-start(f32[8,6,1,128]{3,2,1,0:T(1,128)S(1)} %get-tuple-element.52), channel_id=1, source_target_pairs={{1,0},{2,1},{3,2},{4,3},{5,4},{6,5},{7,6},{8,7},{9,8},{10,9},{11,1... | collective-permute-start | bytes 73736 | tf_op jit(solution)/shard_map/ppermute | solution.py:27
  245.8 6.0 %collective-permute-start.23 = (f32[8,6,1,128]{3,2,1,0:T(1,128)S(1)}, f32[8,6,1,128]{3,2,1,0:T(1,128)S(1)}, u32[]{:S(2)}, u32[]{:S(2)}) collective-permute-start(f32[8,6,1,128]{3,2,1,0:T(1,128)S(1)} %get-tuple-element.53), channel_id=1, source_target_pairs={{0,1},{1,2},{2,3},{3,4},{4,5},{5,6},{6,7},{7,8},{8,9},{9,10},{10,1... | collective-permute-start | bytes 73736 | tf_op jit(solution)/shard_map/ppermute | solution.py:25
  252.0 5.9 %collective-permute-start.24 = (f32[8,1,8,128]{3,2,1,0:T(8,128)S(1)}, f32[8,1,8,128]{3,2,1,0:T(8,128)S(1)}, u32[]{:S(2)}, u32[]{:S(2)}) collective-permute-start(f32[8,1,8,128]{3,2,1,0:T(8,128)S(1)} %get-tuple-element.57), channel_id=1, source_target_pairs={{16,0},{32,16},{48,32},{64,48},{80,64},{96,80},{112,96},{128,112},... | collective-permute-start | bytes 98312 | tf_op jit(solution)/shard_map/ppermute | solution.py:27
  253.3 5.6 %collective-permute-start.25 = (f32[8,1,8,128]{3,2,1,0:T(8,128)S(1)}, f32[8,1,8,128]{3,2,1,0:T(8,128)S(1)}, u32[]{:S(2)}, u32[]{:S(2)}) collective-permute-start(f32[8,1,8,128]{3,2,1,0:T(8,128)S(1)} %get-tuple-element.56), channel_id=1, source_target_pairs={{0,16},{16,32},{32,48},{48,64},{64,80},{80,96},{96,112},{112,128},... | collective-permute-start | bytes 98312 | tf_op jit(solution)/shard_map/ppermute | solution.py:25
  258.9 7.0 %collective-permute-start.26 = (f32[8,6,1,128]{3,2,1,0:T(1,128)S(1)}, f32[8,6,1,128]{3,2,1,0:T(1,128)S(1)}, u32[]{:S(2)}, u32[]{:S(2)}) collective-permute-start(f32[8,6,1,128]{3,2,1,0:T(1,128)S(1)} %get-tuple-element.50), channel_id=1, source_target_pairs={{1,0},{2,1},{3,2},{4,3},{5,4},{6,5},{7,6},{8,7},{9,8},{10,9},{11,1... | collective-permute-start | bytes 73736 | tf_op jit(solution)/shard_map/ppermute | solution.py:27
  260.8 6.0 %collective-permute-start.27 = (f32[8,6,1,128]{3,2,1,0:T(1,128)S(1)}, f32[8,6,1,128]{3,2,1,0:T(1,128)S(1)}, u32[]{:S(2)}, u32[]{:S(2)}) collective-permute-start(f32[8,6,1,128]{3,2,1,0:T(1,128)S(1)} %get-tuple-element.51), channel_id=1, source_target_pairs={{0,1},{1,2},{2,3},{3,4},{4,5},{5,6},{6,7},{7,8},{8,9},{9,10},{10,1... | collective-permute-start | bytes 73736 | tf_op jit(solution)/shard_map/ppermute | solution.py:25
  289.7 17.3 %copy-start.7 = (f32[8,16,256]{2,1,0:T(8,128)S(1)}, f32[8,16,256]{2,1,0:T(8,128)}, u32[]{:S(2)}) copy-start(f32[8,16,256]{2,1,0:T(8,128)} %get-tuple-element.30) | copy-start | bytes 393220
  289.7 17.3 %copy-start.9 = (f32[8,16,256]{2,1,0:T(8,128)S(1)}, f32[8,16,256]{2,1,0:T(8,128)}, u32[]{:S(2)}) copy-start(f32[8,16,256]{2,1,0:T(8,128)} %copy-done.8) | copy-start | bytes 393220
  289.7 17.3 %copy-start.13 = (f32[8,16,256]{2,1,0:T(8,128)S(1)}, f32[8,16,256]{2,1,0:T(8,128)}, u32[]{:S(2)}) copy-start(f32[8,16,256]{2,1,0:T(8,128)} %copy-done.11) | copy-start | bytes 393220
  289.7 17.3 %copy-start.16 = (f32[8,16,256]{2,1,0:T(8,128)S(1)}, f32[8,16,256]{2,1,0:T(8,128)}, u32[]{:S(2)}) copy-start(f32[8,16,256]{2,1,0:T(8,128)} %copy-done.14) | copy-start | bytes 393220
  289.7 17.3 %copy-start.19 = (f32[8,16,256]{2,1,0:T(8,128)S(1)}, f32[8,16,256]{2,1,0:T(8,128)}, u32[]{:S(2)}) copy-start(f32[8,16,256]{2,1,0:T(8,128)} %copy-done.17) | copy-start | bytes 393220
  289.8 6.4 %collective-permute-start.28 = (f32[8,1,16,256]{3,2,1,0:T(8,128)S(1)}, f32[8,1,16,256]{3,2,1,0:T(8,128)S(1)}, u32[]{:S(2)}, u32[]{:S(2)}) collective-permute-start(f32[8,1,16,256]{3,2,1,0:T(8,128)S(1)} %get-tuple-element.43), channel_id=1, source_target_pairs={{16,0},{32,16},{48,32},{64,48},{80,64},{96,80},{112,96},{128,112},... | collective-permute-start | bytes 393224 | tf_op jit(solution)/shard_map/ppermute | solution.py:27
  291.2 6.5 %collective-permute-start.29 = (f32[8,1,16,256]{3,2,1,0:T(8,128)S(1)}, f32[8,1,16,256]{3,2,1,0:T(8,128)S(1)}, u32[]{:S(2)}, u32[]{:S(2)}) collective-permute-start(f32[8,1,16,256]{3,2,1,0:T(8,128)S(1)} %get-tuple-element.42), channel_id=1, source_target_pairs={{0,16},{16,32},{32,48},{48,64},{64,80},{80,96},{96,112},{112,128},... | collective-permute-start | bytes 393224 | tf_op jit(solution)/shard_map/ppermute | solution.py:25
  297.9 7.8 %collective-permute-start.30 = (f32[8,10,1,256]{3,0,2,1:T(8,128)S(1)}, f32[8,10,1,256]{3,0,2,1:T(8,128)S(1)}, u32[]{:S(2)}, u32[]{:S(2)}) collective-permute-start(f32[8,10,1,256]{3,0,2,1:T(8,128)S(1)} %copy.453), channel_id=1, source_target_pairs={{1,0},{2,1},{3,2},{4,3},{5,4},{6,5},{7,6},{8,7},{9,8},{10,9},{11,1... | collective-permute-start | bytes 245768 | tf_op jit(solution)/shard_map/ppermute | solution.py:27
  299.8 7.1 %collective-permute-start.31 = (f32[8,10,1,256]{3,0,2,1:T(8,128)S(1)}, f32[8,10,1,256]{3,0,2,1:T(8,128)S(1)}, u32[]{:S(2)}, u32[]{:S(2)}) collective-permute-start(f32[8,10,1,256]{3,0,2,1:T(8,128)S(1)} %copy.455), channel_id=1, source_target_pairs={{0,1},{1,2},{2,3},{3,4},{4,5},{5,6},{6,7},{7,8},{8,9},{9,10},{10,1... | collective-permute-start | bytes 245768 | tf_op jit(solution)/shard_map/ppermute | solution.py:25
  (5 other events, 10.7 us)
